TPU v7x, 32 devices: a whole 2x2x4 slice. The times are simulated.
32 devices in a mesh: groups: 2 (over x), dp: 16 (over z, y, core).
Axes of the slice: x: 2, y: 2, z: 4, core: 2. Of those that a mesh axis runs over, the one named last changes fastest.
Arguments:
- query: bfloat16 [16384, 4096], P(('groups', 'dp')), parts along dimension 0, may hold values from -6 to 6
- resp_key: bfloat16 [16384, 1024], P(('groups', 'dp')), parts along dimension 0, may hold values from -6 to 6
- resp_value: bfloat16 [16384, 1024], P(('groups', 'dp')), parts along dimension 0, may hold values from -6 to 6
- prompt_key: bfloat16 [2048, 1024], P(('groups', 'dp')), parts along dimension 0, may hold values from -6 to 6
- prompt_value: bfloat16 [2048, 1024], P(('groups', 'dp')), parts along dimension 0, may hold values from -6 to 6
- grad_out: bfloat16 [16384, 4096], P(('groups', 'dp')), parts along dimension 0, may hold values from -6 to 6
- resp_lengths: int32 [32, 4], P(('groups', 'dp')), parts along dimension 0, may hold values from 1 to 256, 512 in all within a row
- resp_prompt: int32 [32], P(('groups', 'dp')), parts along dimension 0, may hold values from 0 to 3
Outputs:
- grad_query: bfloat16 [16384, 4096], P(('groups', 'dp')), parts along dimension 0
- grad_resp_key: bfloat16 [16384, 1024], P(('groups', 'dp')), parts along dimension 0
- grad_resp_value: bfloat16 [16384, 1024], P(('groups', 'dp')), parts along dimension 0
- grad_prompt_key: bfloat16 [2048, 1024], P(('groups', 'dp')), parts along dimension 0
- grad_prompt_value: bfloat16 [2048, 1024], P(('groups', 'dp')), parts along dimension 0
There are 2 independent parts, one for each index of `groups`. A program takes and returns all parts, laid end to end along the dimension named above; each array names one. Nothing has to cross between parts.
Inputs may be any that keep to these rules, and one draw needn't show every extreme that they name: `resp_lengths`: each row sums to 512.
All inputs are finite; a program needn't handle non-finite values.
Results may differ from a plain program's by a relative error of at most 0.0092.
Values may be sent and summed in bfloat16 or wider, within the bound.
A program may use at most 128 MiB of HBM per device.

v0:
```python
import jax
import jax.numpy as jnp
from jax import lax
from jax.sharding import PartitionSpec as P

HEADS = 32
KV_HEADS = 8
D_HEAD = 128


def allowed_mask(lengths, prompt_rows, rows):
    ends = jnp.cumsum(lengths)
    place = jnp.arange(rows, dtype=jnp.int32)
    segment = jnp.sum((place[:, None] >= ends[None, :]).astype(jnp.int32), axis=1)
    own = (segment[:, None] == segment[None, :]) & (place[None, :] <= place[:, None])
    return jnp.concatenate([jnp.ones((rows, prompt_rows), bool), own], axis=1)


def head_step(mask, q_head, k_head, v_head, g_head):
    scale = D_HEAD ** (-0.5)
    scores = jnp.einsum("qgd,sd->gqs", q_head, k_head, preferred_element_type=jnp.float32) * scale
    scores = jnp.where(mask[None], scores, -1e30)
    top = jnp.max(scores, axis=-1, keepdims=True)
    expo = jnp.exp(scores - top)
    probs = expo / jnp.sum(expo, axis=-1, keepdims=True)
    weights = probs.astype(jnp.bfloat16)
    out = jnp.einsum("gqs,sd->qgd", weights, v_head, preferred_element_type=jnp.float32)
    dprob = jnp.einsum("qgd,sd->gqs", g_head, v_head, preferred_element_type=jnp.float32)
    delta = jnp.sum(g_head.astype(jnp.float32) * out, axis=-1).transpose(1, 0)[:, :, None]
    dscore = (probs * (dprob - delta) * scale).astype(jnp.bfloat16)
    grad_q = jnp.einsum("gqs,sd->qgd", dscore, k_head, preferred_element_type=jnp.float32).astype(
        jnp.bfloat16
    )
    grad_k = jnp.einsum("gqs,qgd->sd", dscore, q_head, preferred_element_type=jnp.float32)
    grad_v = jnp.einsum("gqs,qgd->sd", weights, g_head, preferred_element_type=jnp.float32)
    return (grad_q, grad_k, grad_v)


def prompt_part(stacked, count, first, length):
    wanted = jnp.arange(count, dtype=jnp.int32) - first
    inside = (wanted >= 0) & (wanted < length)
    picked = jnp.take(stacked, jnp.clip(wanted, 0, length - 1), axis=0)
    return jnp.where(inside[:, None], picked, jnp.zeros_like(picked))


def shards(
    query, resp_key, resp_value, prompt_key, prompt_value, grad_out, resp_lengths, resp_prompt
):
    rows = query.shape[0]
    own_rows = prompt_key.shape[0]
    quarters = 4
    prompt_len = quarters * own_rows
    width = KV_HEADS * D_HEAD
    group = HEADS // KV_HEADS
    first = resp_prompt[0] * prompt_len
    all_keys, all_values = (
        lax.all_gather(prompt_key, "dp", axis=0, tiled=True),
        lax.all_gather(prompt_value, "dp", axis=0, tiled=True),
    )
    mine_k = lax.dynamic_slice_in_dim(all_keys, first, prompt_len, 0)
    mine_v = lax.dynamic_slice_in_dim(all_values, first, prompt_len, 0)
    keys = jnp.concatenate([mine_k, resp_key], 0).reshape(-1, KV_HEADS, D_HEAD).transpose(1, 0, 2)
    values = (
        jnp.concatenate([mine_v, resp_value], 0).reshape(-1, KV_HEADS, D_HEAD).transpose(1, 0, 2)
    )
    queries = query.reshape(rows, KV_HEADS, group, D_HEAD).transpose(1, 0, 2, 3)
    grads = grad_out.reshape(rows, KV_HEADS, group, D_HEAD).transpose(1, 0, 2, 3)
    mask = allowed_mask(resp_lengths[0], prompt_len, rows)
    grad_q, grad_k, grad_v = lax.map(
        lambda xs: head_step(mask, *xs), (queries, keys, values, grads)
    )
    grad_q = grad_q.transpose(1, 0, 2, 3).reshape(rows, HEADS * D_HEAD)
    grad_k = grad_k.transpose(1, 0, 2).reshape(-1, width)
    grad_v = grad_v.transpose(1, 0, 2).reshape(-1, width)
    stacked = jnp.concatenate([grad_k[:prompt_len], grad_v[:prompt_len]], 1)
    summed = lax.psum_scatter(
        prompt_part(stacked, own_rows * lax.axis_size("dp"), first, prompt_len),
        "dp",
        scatter_dimension=0,
        tiled=True,
    )
    return (
        grad_q,
        grad_k[prompt_len:].astype(jnp.bfloat16),
        grad_v[prompt_len:].astype(jnp.bfloat16),
        summed[:, :width].astype(jnp.bfloat16),
        summed[:, width:].astype(jnp.bfloat16),
    )


def solution(mesh):
    return jax.shard_map(
        shards,
        mesh=mesh,
        in_specs=(
            P(("groups", "dp"), None),
            P(("groups", "dp"), None),
            P(("groups", "dp"), None),
            P(("groups", "dp"), None),
            P(("groups", "dp"), None),
            P(("groups", "dp"), None),
            P(("groups", "dp"), None),
            P(("groups", "dp")),
        ),
        out_specs=(
            P(("groups", "dp"), None),
            P(("groups", "dp"), None),
            P(("groups", "dp"), None),
            P(("groups", "dp"), None),
            P(("groups", "dp"), None),
        ),
        check_vma=False,
    )
```

profile of v0, /device:TPU:0, one launch (start us, length us, event | category | flops | bytes accessed | tf_op | source)
XLA Modules:
  0.0 459.3 jit_solution(9274598424682912764)
XLA Ops:
  12.6 6.4 %copy.70 = bf16[512,4096]{0,1:T(8,128)(2,1)} copy(bf16[512,4096]{1,0:T(8,128)(2,1)} %param.10) | data formatting | bytes 8388608 | tf_op args[0]
  19.0 6.6 %copy.73 = bf16[512,4096]{0,1:T(8,128)(2,1)} copy(bf16[512,4096]{1,0:T(8,128)(2,1)} %param.15) | data formatting | bytes 8388608 | tf_op args[5]
  26.5 27.8 %all-gather.3.cloned.1.call-done = bf16[1024,1024]{1,0:T(8,128)(2,1)} async-done(((bf16[64,1024]{1,0:T(8,128)(2,1)}), bf16[1024,1024]{1,0:T(8,128)(2,1)}) %all-gather.3.cloned.1.call-update) | async-done | bytes 2097168 | tf_op jit(solution)/shard_map/all_gather | solution.py:57
  54.3 42.4 %all-gather.5.cloned.1.call-done = bf16[1024,1024]{1,0:T(8,128)(2,1)} async-done(((bf16[64,1024]{1,0:T(8,128)(2,1)}), bf16[1024,1024]{1,0:T(8,128)(2,1)}) %all-gather.5.cloned.1.call-update) | async-done | bytes 2097168 | tf_op jit(solution)/shard_map/all_gather | solution.py:58
  102.8 228.7 %while.14 = (s32[]{:T(128)}, bf16[8,512,4,128]{1,3,2,0:T(8,128)(2,1)}, f32[8,768,128]{2,1,0:T(8,128)}, f32[8,768,128]{2,1,0:T(8,128)}, bf16[8,768,128]{1,2,0:T(8...) while((s32[]{:T(128)}, ...), condition=%wide.region_6.7_spmd, body=%wide.region_2.6_spmd.sunk | while | flops 2434267904 | bytes 45004392 | solution.py:69
  102.8 6.2 %fusion.112 = (f32[4,512]{1,0:T(4,128)S(1)}, f32[4,512,768]{1,2,0:T(8,128)}) fusion(pred[512,768]{0,1:T(8,128)(4,1)S(1)} %get-tuple-element.194, bf16[8,512,4,128]{1,3,2,0:T(8,128)(2,1)} %get-tuple-element.195, s32[]{:T(128)} %get-tuple-element.179, bf16[8,768,128]{1,2,0:T(8,128)(2,1)} %get-tuple-element.193), kind=kOutput, calls=%fused_computation.83.clone.1 | convolution fusion | flops 408945408 | bytes 7414784 | tf_op jit(solution)/shard_map/while/body/eval_jaxpr/sub | solution.py:24
  109.0 3.7 fusion.113
  119.3 4.1 fusion.115
  125.8 2.8 fusion.117
  128.6 2.8 fusion.118
  131.4 6.2 %fusion.112 = (f32[4,512]{1,0:T(4,128)S(1)}, f32[4,512,768]{1,2,0:T(8,128)}) fusion(pred[512,768]{0,1:T(8,128)(4,1)S(1)} %get-tuple-element.194, bf16[8,512,4,128]{1,3,2,0:T(8,128)(2,1)} %get-tuple-element.195, s32[]{:T(128)} %get-tuple-element.179, bf16[8,768,128]{1,2,0:T(8,128)(2,1)} %get-tuple-element.193), kind=kOutput, calls=%fused_computation.83.clone.1 | convolution fusion | flops 408945408 | bytes 7414784 | tf_op jit(solution)/shard_map/while/body/eval_jaxpr/sub | solution.py:24
  137.6 3.7 fusion.113
  148.0 4.1 fusion.115
  154.4 2.8 fusion.117
  157.2 2.8 fusion.118
  160.0 6.2 %fusion.112 = (f32[4,512]{1,0:T(4,128)S(1)}, f32[4,512,768]{1,2,0:T(8,128)}) fusion(pred[512,768]{0,1:T(8,128)(4,1)S(1)} %get-tuple-element.194, bf16[8,512,4,128]{1,3,2,0:T(8,128)(2,1)} %get-tuple-element.195, s32[]{:T(128)} %get-tuple-element.179, bf16[8,768,128]{1,2,0:T(8,128)(2,1)} %get-tuple-element.193), kind=kOutput, calls=%fused_computation.83.clone.1 | convolution fusion | flops 408945408 | bytes 7414784 | tf_op jit(solution)/shard_map/while/body/eval_jaxpr/sub | solution.py:24
  166.2 3.7 fusion.113
  176.5 4.1 fusion.115
  183.0 2.8 fusion.117
  188.5 6.2 %fusion.112 = (f32[4,512]{1,0:T(4,128)S(1)}, f32[4,512,768]{1,2,0:T(8,128)}) fusion(pred[512,768]{0,1:T(8,128)(4,1)S(1)} %get-tuple-element.194, bf16[8,512,4,128]{1,3,2,0:T(8,128)(2,1)} %get-tuple-element.195, s32[]{:T(128)} %get-tuple-element.179, bf16[8,768,128]{1,2,0:T(8,128)(2,1)} %get-tuple-element.193), kind=kOutput, calls=%fused_computation.83.clone.1 | convolution fusion | flops 408945408 | bytes 7414784 | tf_op jit(solution)/shard_map/while/body/eval_jaxpr/sub | solution.py:24
  194.8 3.7 fusion.113
  205.1 4.1 fusion.115
  211.6 2.8 fusion.117
  217.1 6.2 %fusion.112 = (f32[4,512]{1,0:T(4,128)S(1)}, f32[4,512,768]{1,2,0:T(8,128)}) fusion(pred[512,768]{0,1:T(8,128)(4,1)S(1)} %get-tuple-element.194, bf16[8,512,4,128]{1,3,2,0:T(8,128)(2,1)} %get-tuple-element.195, s32[]{:T(128)} %get-tuple-element.179, bf16[8,768,128]{1,2,0:T(8,128)(2,1)} %get-tuple-element.193), kind=kOutput, calls=%fused_computation.83.clone.1 | convolution fusion | flops 408945408 | bytes 7414784 | tf_op jit(solution)/shard_map/while/body/eval_jaxpr/sub | solution.py:24
  223.3 3.7 fusion.113
  233.7 4.1 fusion.115
  242.9 2.8 fusion.118
  245.7 6.2 %fusion.112 = (f32[4,512]{1,0:T(4,128)S(1)}, f32[4,512,768]{1,2,0:T(8,128)}) fusion(pred[512,768]{0,1:T(8,128)(4,1)S(1)} %get-tuple-element.194, bf16[8,512,4,128]{1,3,2,0:T(8,128)(2,1)} %get-tuple-element.195, s32[]{:T(128)} %get-tuple-element.179, bf16[8,768,128]{1,2,0:T(8,128)(2,1)} %get-tuple-element.193), kind=kOutput, calls=%fused_computation.83.clone.1 | convolution fusion | flops 408945408 | bytes 7414784 | tf_op jit(solution)/shard_map/while/body/eval_jaxpr/sub | solution.py:24
  251.9 3.7 fusion.113
  262.3 4.1 fusion.115
  268.8 2.8 fusion.117
  271.6 2.8 fusion.118
  274.3 6.2 %fusion.112 = (f32[4,512]{1,0:T(4,128)S(1)}, f32[4,512,768]{1,2,0:T(8,128)}) fusion(pred[512,768]{0,1:T(8,128)(4,1)S(1)} %get-tuple-element.194, bf16[8,512,4,128]{1,3,2,0:T(8,128)(2,1)} %get-tuple-element.195, s32[]{:T(128)} %get-tuple-element.179, bf16[8,768,128]{1,2,0:T(8,128)(2,1)} %get-tuple-element.193), kind=kOutput, calls=%fused_computation.83.clone.1 | convolution fusion | flops 408945408 | bytes 7414784 | tf_op jit(solution)/shard_map/while/body/eval_jaxpr/sub | solution.py:24
  280.6 3.7 fusion.113
  290.9 4.1 fusion.115
  297.4 2.8 fusion.117
  300.1 2.8 fusion.118
  302.9 6.2 %fusion.112 = (f32[4,512]{1,0:T(4,128)S(1)}, f32[4,512,768]{1,2,0:T(8,128)}) fusion(pred[512,768]{0,1:T(8,128)(4,1)S(1)} %get-tuple-element.194, bf16[8,512,4,128]{1,3,2,0:T(8,128)(2,1)} %get-tuple-element.195, s32[]{:T(128)} %get-tuple-element.179, bf16[8,768,128]{1,2,0:T(8,128)(2,1)} %get-tuple-element.193), kind=kOutput, calls=%fused_computation.83.clone.1 | convolution fusion | flops 408945408 | bytes 7414784 | tf_op jit(solution)/shard_map/while/body/eval_jaxpr/sub | solution.py:24
  309.1 3.7 fusion.113
  319.5 4.1 fusion.115
  325.9 2.8 fusion.117
  328.7 2.8 fusion.118
  334.3 6.8 %gather_fusion = f32[1024,2048]{1,0:T(8,128)} fusion(f32[256,2048]{1,0:T(8,128)S(1)} %pad_maximum_fusion, s32[1024]{0:T(1024)S(1)} %broadcast_clamp_fusion), kind=kCustom, calls=%fused_computation | custom fusion | bytes 16781312 | tf_op jit(solution)/shard_map/jit(_take)/gather | solution.py:42
  341.1 6.3 %select_select_fusion = f32[1024,2048]{1,0:T(8,128)} fusion(f32[1024,2048]{1,0:T(8,128)} %gather_fusion, pred[1024]{0:T(1024)(128)(4,1)S(1)} %get-tuple-element.106, pred[1024]{0:T(1024)(128)(4,1)S(1)} %copy-done), kind=kLoop, calls=%fused_computation.53 | loop fusion | flops 4194304 | bytes 16779264 | tf_op jit(solution)/shard_map/jit(_where)/select_n | solution.py:43
  347.4 6.3 %copy.90 = bf16[512,4096]{1,0:T(8,128)(2,1)} copy(bf16[512,4096]{0,1:T(8,128)(2,1)} %bitcast.182) | data formatting | bytes 8388608 | tf_op jit(solution)/shard_map/reshape | solution.py:72
  353.7 3.0 copy_bitcast_fusion.2
  356.7 2.9 copy_bitcast_fusion.3
  359.6 91.4 %reduce-scatter.2.cloned.1.call-done = f32[64,2048]{1,0:T(8,128)} async-done(((f32[1024,2048]{1,0:T(8,128)}), f32[64,2048]{1,0:T(8,128)}) %reduce-scatter.2.cloned.1.call-update) | async-done | bytes 524304 | tf_op jit(solution)/shard_map/reduce_scatter | solution.py:76
  (67 shorter events, 96.4 us)
Async XLA Ops:
  7.2 5.2 %copy-start.1 = (s32[1,4]{1,0:T(1,128)S(1)}, s32[1,4]{1,0:T(1,128)}, u32[]{:S(2)}) copy-start(s32[1,4]{1,0:T(1,128)} %param.16) | copy-start | bytes 52
  7.2 47.1 %all-gather.3.cloned.1.call-start = ((), (), s32[]{:S(2)}) async-start(), calls=%async_computation.1 | async-start | bytes 2228224 | tf_op jit(solution)/shard_map/all_gather | solution.py:57
  7.9 88.8 %all-gather.5.cloned.1.call-start = ((), (), s32[]{:S(2)}) async-start(), calls=%async_computation.2 | async-start | bytes 2228224 | tf_op jit(solution)/shard_map/all_gather | solution.py:58
  8.7 442.3 %reduce-scatter.2.cloned.1.call-start = ((), (), s32[]{:S(2)}) async-start(), calls=%async_computation.3 | async-start | bytes 8912896 | tf_op jit(solution)/shard_map/reduce_scatter | solution.py:76
  334.3 6.8 %copy-start = (pred[1024]{0:T(1024)(128)(4,1)S(1)}, pred[1024]{0:T(1024)(128)(4,1)}, u32[]{:S(2)}) copy-start(pred[1024]{0:T(1024)(128)(4,1)} %get-tuple-element.107) | copy-start | bytes 3076
Sparse Core Ops, SparseCore 0:
  10.2 44.0 all-gather.2
  56.5 40.1 all-gather.4
  347.5 103.4 reduce-scatter.1
where the time goes:
time: 463 us; the launch traced here: 459 us
  matrix products  168 us (36%)
  waiting for transfers between devices  163 us (35%)
  local copies, waits for them, and re-layouts  72.3 us (16%)
  other arithmetic  41.6 us (9%)
  between operations  14.5 us (3%)
    reduce_scatter x1, waiting for transfers between devices, shards(): lax.psum_scatter(prompt_part(stacked, own_rows * lax.axis_size('dp'), fir...  91.4 us
    sub x8, matrix products, head_step(): expo = jnp.exp(scores - top)  49.8 us
    all_gather x1, waiting for transfers between devices, shards(): lax.all_gather(prompt_value, 'dp', axis=0, tiled=True)  42.4 us
    dot_general x8, matrix products, head_step(): jnp.einsum('qgd,sd->gqs', g_head, v_head, preferred_element_type=jnp.floa...  33.2 us
    dynamic_slice x16, local copies, waits for them, and re-layouts, shards(): lax.map(lambda xs: head_step(mask, *xs), (queries, keys, values, grads))  31.3 us
    convert_element_type x8, other arithmetic, head_step(): weights = probs.astype(jnp.bfloat16)  29.5 us
    all_gather x1, waiting for transfers between devices, shards(): lax.all_gather(prompt_key, 'dp', axis=0, tiled=True)  27.8 us
    dot_general x8, matrix products, head_step(): jnp.einsum('gqs,qgd->sd', dscore, q_head, preferred_element_type=jnp.floa...  22.1 us
  transfers between devices with their start and end apart: 3, of which 3 were waited for; matrix products, arithmetic and copies ran while one was open for 6% of the time, Pallas kernels for 0%

commit v1 on v0

v1 whole, which is shorter than its diff:
```python
import functools

import jax
import jax.numpy as jnp
from jax import lax
from jax.experimental import pallas as pl
from jax.experimental.pallas import tpu as pltpu
from jax.sharding import PartitionSpec as P

HEADS = 32
KV_HEADS = 8
D_HEAD = 128
GROUP = HEADS // KV_HEADS
RESP_MAX = 256
QB = 128
SCALE = D_HEAD ** (-0.5)
LOG2E = 1.4426950408889634
F32 = jnp.float32
BF16 = jnp.bfloat16


def dot(a, b, ca, cb):
    return lax.dot_general(a, b, (((ca,), (cb,)), ((), ())), preferred_element_type=F32)


def fill_bias(lens, bias_ref):
    rows = bias_ref.shape[0]
    place = lax.broadcasted_iota(jnp.int32, (1, rows), 1)
    begin = jnp.zeros((1, rows), jnp.int32)
    end = jnp.int32(0)
    for i in range(len(lens)):
        end = end + lens[i]
        begin = jnp.where(place >= end, end, begin)
    key = lax.broadcasted_iota(jnp.int32, (rows, rows), 0)
    ok = (key >= begin) & (key <= place)
    bias_ref[...] = jnp.where(ok, 0.0, -1e30)


def head_grads(q_ref, g_ref, pk, pv, rk_ref, rv_ref, bias_ref, gq_ref, acc_k, acc_v, lane0):
    rows = bias_ref.shape[0]
    plen = pk.shape[0]
    back = -(-(RESP_MAX - 1) // QB) * QB
    acc_k[...] = jnp.zeros_like(acc_k)
    acc_v[...] = jnp.zeros_like(acc_v)
    for q0 in range(0, rows, QB):
        lo, hi = max(0, q0 - back), q0 + QB

        def stacked(ref):
            return jnp.concatenate(
                [ref[q0:hi, j * D_HEAD:(j + 1) * D_HEAD] for j in range(GROUP)], 0
            )

        q, g = stacked(q_ref), stacked(g_ref)
        k = jnp.concatenate([pk, rk_ref[lo:hi, :]], 0)
        v = jnp.concatenate([pv, rv_ref[lo:hi, :]], 0)
        s = dot(k, q, 1, 1)
        bias = bias_ref[lo:hi, q0:hi]
        s_p = s[:plen]
        s_r = s[plen:] + jnp.concatenate([bias] * GROUP, 1)
        top = jnp.maximum(
            jnp.max(s_p, axis=0, keepdims=True), jnp.max(s_r, axis=0, keepdims=True)
        )
        e = jnp.concatenate([s_p, s_r], 0) - top
        e = jnp.exp2(e * (SCALE * LOG2E))
        inv = 1.0 / jnp.sum(e, axis=0, keepdims=True)
        dp = dot(v, g, 1, 1)
        delta = jnp.sum(e * dp, axis=0, keepdims=True) * inv
        p = e * inv
        w = p.astype(BF16)
        ds = (p * (dp - delta)).astype(BF16)
        gv = dot(w, g, 1, 0)
        gk = dot(ds, q, 1, 0)
        acc_v[:plen, :] += gv[:plen]
        acc_v[plen + lo:plen + hi, :] += gv[plen:]
        acc_k[:plen, :] += gk[:plen]
        acc_k[plen + lo:plen + hi, :] += gk[plen:]
        gq = dot(k, ds, 0, 0) * SCALE
        for j in range(GROUP):
            gq_ref[q0:hi, j * D_HEAD:(j + 1) * D_HEAD] = (
                gq[:, j * QB:(j + 1) * QB].T.astype(BF16)
            )


def kernel(which, lens_ref, q_ref, g_ref, pk_ref, pv_ref, rk_ref, rv_ref,
           gq_ref, grk_ref, grv_ref, gpk_ref, gpv_ref, bias_ref, acc_k, acc_v):
    @pl.when(pl.program_id(0) == 0)
    def _():
        fill_bias([lens_ref[0, i] for i in range(lens_ref.shape[1])], bias_ref)

    plen = pk_ref.shape[0]
    head_grads(q_ref, g_ref, pk_ref[...], pv_ref[...], rk_ref, rv_ref, bias_ref, gq_ref,
               acc_k, acc_v, 0)
    gpk_ref[...] = (acc_k[:plen, :] * SCALE).astype(BF16)
    gpv_ref[...] = acc_v[:plen, :].astype(BF16)
    grk_ref[...] = (acc_k[plen:, :] * SCALE).astype(BF16)
    grv_ref[...] = acc_v[plen:, :].astype(BF16)


def attention(which, lengths, query, grad_out, keys, resp_key, resp_value, plen):
    rows = query.shape[0]
    width = KV_HEADS * D_HEAD
    wide = pl.BlockSpec((rows, GROUP * D_HEAD), lambda h, w: (0, h))
    own = pl.BlockSpec((rows, D_HEAD), lambda h, w: (0, h))
    out_p = pl.BlockSpec((plen, D_HEAD), lambda h, w: (0, h))
    sds = jax.ShapeDtypeStruct
    return pl.pallas_call(
        kernel,
        grid_spec=pltpu.PrefetchScalarGridSpec(
            num_scalar_prefetch=1,
            grid=(KV_HEADS,),
            in_specs=[
                pl.BlockSpec(memory_space=pltpu.SMEM),
                wide,
                wide,
                pl.BlockSpec((plen, D_HEAD), lambda h, w: (w[0], h)),
                pl.BlockSpec((plen, D_HEAD), lambda h, w: (w[0], h + KV_HEADS)),
                own,
                own,
            ],
            out_specs=[wide, own, own, out_p, out_p],
            scratch_shapes=[
                pltpu.VMEM((rows, rows), F32),
                pltpu.VMEM((plen + rows, D_HEAD), F32),
                pltpu.VMEM((plen + rows, D_HEAD), F32),
            ],
        ),
        out_shape=[
            sds((rows, HEADS * D_HEAD), BF16),
            sds((rows, width), BF16),
            sds((rows, width), BF16),
            sds((plen, width), BF16),
            sds((plen, width), BF16),
        ],
        compiler_params=pltpu.CompilerParams(
            dimension_semantics=("arbitrary",), vmem_limit_bytes=40 * 1024 * 1024
        ),
    )(which, lengths, query, grad_out, keys, keys, resp_key, resp_value)


def shards(
    query, resp_key, resp_value, prompt_key, prompt_value, grad_out, resp_lengths, resp_prompt
):
    own_rows = prompt_key.shape[0]
    plen = 4 * own_rows
    width = KV_HEADS * D_HEAD
    every = lax.all_gather(
        jnp.concatenate([prompt_key, prompt_value], 1), "dp", axis=0, tiled=True
    )
    gq, grk, grv, gpk, gpv = attention(
        resp_prompt, resp_lengths, query, grad_out, every, resp_key, resp_value, plen
    )
    terms = jnp.zeros((own_rows * lax.axis_size("dp"), 2 * width), BF16)
    terms = lax.dynamic_update_slice(
        terms, jnp.concatenate([gpk, gpv], 1), (resp_prompt[0] * plen, 0)
    )
    summed = lax.psum_scatter(terms, "dp", scatter_dimension=0, tiled=True)
    return gq, grk, grv, summed[:, :width], summed[:, width:]


def solution(mesh):
    rows = P(("groups", "dp"), None)
    return jax.shard_map(
        shards,
        mesh=mesh,
        in_specs=(rows,) * 7 + (P(("groups", "dp")),),
        out_specs=(rows,) * 5,
        check_vma=False,
    )
```

time: 463 us -> 193 us (0.42)
  matrix products: 168 us -> 0 us
  local copies, waits for them, and re-layouts: 72.3 us -> 11.6 us
  other arithmetic: 41.6 us -> 2.75 us
  Pallas kernels: 0 us -> 37.5 us
  waiting for transfers between devices: 163 us -> 126 us
    dot_general x40 -> x0, matrix products: 118 us -> none  [the longest x8 33.2 us: head_step(): jnp.einsum('qgd,sd->gqs', g_head, v_head, preferred_element_type=jnp.floa...]
    sub x8 -> x0, matrix products: 49.8 us -> none  [head_step(): expo = jnp.exp(scores - top)]
    pallas_call x0 -> x1, Pallas kernels: none -> 37.5 us  [attention(): pl.pallas_call(kernel, grid_spec=pltpu.PrefetchScalarGridSpec(num_scalar_...]
    dynamic_slice x17 -> x0, local copies, waits for them, and re-layouts: 32.6 us -> none  [the longest x16 31.3 us: shards(): lax.map(lambda xs: head_step(mask, *xs), (queries, keys, values, grads))]
    convert_element_type x8 -> x0, other arithmetic: 29.5 us -> none  [head_step(): weights = probs.astype(jnp.bfloat16)]
    reduce_scatter x1, waiting for transfers between devices: 91.4 us -> 71.1 us  [shards(): summed = lax.psum_scatter(terms, 'dp', scatter_dimension=0, tiled=True)]
    all_gather x2 -> x1, waiting for transfers between devices: 70.1 us -> 54.4 us  [shards(): lax.all_gather(jnp.concatenate([prompt_key, prompt_value], 1), 'dp', axis...]
    unnamed x10, local copies, waits for them, and re-layouts: 17.2 us -> 7.48 us
  transfers between devices with their start and end apart: 3 -> 2, of which waited for: 3 -> 2; matrix products, arithmetic and copies ran while one was open for 6% -> 0% of each run, Pallas kernels for 0% -> 0%
where the time goes in v1:
time: 193 us; the launch traced here: 192 us
  waiting for transfers between devices  126 us (65%)
  Pallas kernels  37.5 us (19%)
  between operations  14.7 us (8%)
  local copies, waits for them, and re-layouts  11.6 us (6%)
  other arithmetic  2.75 us (1%)
    reduce_scatter x1, waiting for transfers between devices, shards(): summed = lax.psum_scatter(terms, 'dp', scatter_dimension=0, tiled=True)  71.1 us
    all_gather x1, waiting for transfers between devices, shards(): lax.all_gather(jnp.concatenate([prompt_key, prompt_value], 1), 'dp', axis...  54.4 us
    pallas_call x1, Pallas kernels, attention(): pl.pallas_call(kernel, grid_spec=pltpu.PrefetchScalarGridSpec(num_scalar_...  37.5 us
    unnamed x10, local copies, waits for them, and re-layouts  7.48 us
  transfers between devices with their start and end apart: 2, of which 2 were waited for; matrix products, arithmetic and copies ran while one was open for 0% of the time, Pallas kernels for 0%

profile of v1, /device:TPU:0, one launch (start us, length us, event | category | flops | bytes accessed | tf_op | source)
XLA Modules:
  0.0 192.1 jit_solution(9256830425706052690)
XLA Ops:
  7.2 0.0 all-gather.2.cloned.1.call-start
  7.2 1.7 pad_maximum_fusion
  8.9 0.0 all-gather.2.cloned.1.call-update
  8.9 0.0 reduce-scatter.2.cloned.1.call-start
  9.6 54.4 %all-gather.2.cloned.1.call-done.pk_ref.pv_ref = bf16[1024,2048]{1,0:T(8,128)(2,1)} async-done(((bf16[64,2048]{1,0:T(8,128)(2,1)}), bf16[1024,2048]{1,0:T(8,128)(2,1)}) %all-gather.2.cloned.1.call-update) | async-done | bytes 4194320 | tf_op jit(solution)/shard_map/all_gather | solution.py:146
  64.0 0.0 copy-start
  64.0 2.2 %copy-done = bf16[512,4096]{1,0:T(8,128)(2,1)S(1)} copy-done((bf16[512,4096]{1,0:T(8,128)(2,1)S(1)}, bf16[512,4096]{1,0:T(8,128)(2,1)}, u32[]{:S(2)}) %copy-start) | copy-done | bytes 4194328
  66.2 0.0 copy-start.1
  66.2 2.2 %copy-done.1 = bf16[512,4096]{1,0:T(8,128)(2,1)S(1)} copy-done((bf16[512,4096]{1,0:T(8,128)(2,1)S(1)}, bf16[512,4096]{1,0:T(8,128)(2,1)}, u32[]{:S(2)}) %copy-start.1) | copy-done | bytes 4194328
  68.4 0.0 copy-start.2
  68.4 1.2 copy-done.2
  69.6 0.0 copy-start.3
  69.6 1.2 copy-done.3
  70.9 0.0 copy-start.4
  70.9 0.7 copy-done.4
  71.5 37.5 %shard_map.119 = (bf16[512,4096]{1,0:T(8,128)(2,1)}, bf16[512,1024]{1,0:T(8,128)(2,1)}, bf16[512,1024]{1,0:T(8,128)(2,1)}, bf16[256,1024]{1,0:T(8,128)(2,1)S(1)}, bf16[256,1024]{1,0:T(8,128)(2,1)S(1)}) custom-call(s32[1]{0:T(128)S(6)} %copy.14.which, s32[1,4]{1,0:T(1,128)S(1)} %copy-done.4, bf16[512,4096]{1,0:T(8,128)(2,1)S(1)} %copy-done, ...), custom_call_target="tpu_custom_call" | custom-call | tf_op jit(solution)/shard_map/pallas_call | solution.py:106
  109.0 2.5 %broadcast_in_dim.3 = bf16[1024,2048]{1,0:T(8,128)(2,1)} broadcast(bf16[]{:T(256)} %constant.1.clone.1), dimensions={} | broadcast | bytes 4194306 | tf_op jit(solution)/shard_map/broadcast_in_dim | solution.py:152
  111.4 1.1 maximum_dynamic-update-slice_fusion
  112.5 0.0 reduce-scatter.2.cloned.1.call-update
  112.5 71.1 %reduce-scatter.2.cloned.1.call-done = bf16[64,2048]{1,0:T(8,128)(2,1)} async-done(((bf16[1024,2048]{1,0:T(8,128)(2,1)}), bf16[64,2048]{1,0:T(8,128)(2,1)}) %reduce-scatter.2.cloned.1.call-update) | async-done | bytes 262160 | tf_op jit(solution)/shard_map/reduce_scatter | solution.py:156
  183.6 1.7 fusion
Async XLA Ops:
  7.2 56.9 %all-gather.2.cloned.1.call-start = ((), (), s32[]{:S(2)}) async-start(), calls=%async_computation.1 | async-start | bytes 4456448 | tf_op jit(solution)/shard_map/all_gather | solution.py:146
  8.9 174.7 %reduce-scatter.2.cloned.1.call-start = ((), (), s32[]{:S(2)}) async-start(), calls=%async_computation.2 | async-start | bytes 4456448 | tf_op jit(solution)/shard_map/reduce_scatter | solution.py:156
  64.0 2.2 %copy-start = (bf16[512,4096]{1,0:T(8,128)(2,1)S(1)}, bf16[512,4096]{1,0:T(8,128)(2,1)}, u32[]{:S(2)}) copy-start(bf16[512,4096]{1,0:T(8,128)(2,1)} %q_ref.1) | copy-start | bytes 12582916
  66.2 2.2 %copy-start.1 = (bf16[512,4096]{1,0:T(8,128)(2,1)S(1)}, bf16[512,4096]{1,0:T(8,128)(2,1)}, u32[]{:S(2)}) copy-start(bf16[512,4096]{1,0:T(8,128)(2,1)} %g_ref.1) | copy-start | bytes 12582916
  68.4 1.2 copy-start.2
  69.6 1.2 copy-start.3
  70.9 0.7 copy-start.4
Sparse Core Ops, SparseCore 0:
  10.7 53.2 all-gather.1
  112.6 70.9 reduce-scatter.1

commit v2 on v1

v2 whole, which is shorter than its diff:
```python
import jax
import jax.numpy as jnp
from jax import lax
from jax.experimental import pallas as pl
from jax.experimental.pallas import tpu as pltpu
from jax.sharding import PartitionSpec as P

HEADS = 32
KV_HEADS = 8
D_HEAD = 128
GROUP = HEADS // KV_HEADS
RESP_MAX = 256
QB = 128
SCALE = D_HEAD ** (-0.5)
LOG2E = 1.4426950408889634
F32 = jnp.float32
BF16 = jnp.bfloat16


def dot(a, b, ca, cb):
    return lax.dot_general(a, b, (((ca,), (cb,)), ((), ())), preferred_element_type=F32)


def fill_bias(lens, bias_ref):
    rows = bias_ref.shape[0]
    place = lax.broadcasted_iota(jnp.int32, (1, rows), 1)
    begin = jnp.zeros((1, rows), jnp.int32)
    end = jnp.int32(0)
    for i in range(len(lens)):
        end = end + lens[i]
        begin = jnp.where(place >= end, end, begin)
    key = lax.broadcasted_iota(jnp.int32, (rows, rows), 0)
    ok = (key >= begin) & (key <= place)
    bias_ref[...] = jnp.where(ok, 0.0, -1e30)


def head_grads(q_ref, g_ref, pk, pv, rk_ref, rv_ref, bias_ref, gq_ref, acc_k, acc_v, lane0):
    rows = bias_ref.shape[0]
    plen = pk.shape[0]
    back = -(-(RESP_MAX - 1) // QB) * QB
    acc_k[...] = jnp.zeros_like(acc_k)
    acc_v[...] = jnp.zeros_like(acc_v)
    for q0 in range(0, rows, QB):
        lo, hi = max(0, q0 - back), q0 + QB

        def stacked(ref):
            return jnp.concatenate(
                [ref[q0:hi, j * D_HEAD:(j + 1) * D_HEAD] for j in range(GROUP)], 0
            )

        q, g = stacked(q_ref), stacked(g_ref)
        k = jnp.concatenate([pk, rk_ref[lo:hi, :]], 0)
        v = jnp.concatenate([pv, rv_ref[lo:hi, :]], 0)
        s = dot(k, q, 1, 1)
        bias = bias_ref[lo:hi, q0:hi]
        s_p = s[:plen]
        s_r = s[plen:] + jnp.concatenate([bias] * GROUP, 1)
        top = jnp.maximum(
            jnp.max(s_p, axis=0, keepdims=True), jnp.max(s_r, axis=0, keepdims=True)
        )
        e = jnp.concatenate([s_p, s_r], 0) - top
        e = jnp.exp2(e * (SCALE * LOG2E))
        inv = 1.0 / jnp.sum(e, axis=0, keepdims=True)
        dp = dot(v, g, 1, 1)
        delta = jnp.sum(e * dp, axis=0, keepdims=True) * inv
        p = e * inv
        w = p.astype(BF16)
        ds = (p * (dp - delta)).astype(BF16)
        gv = dot(w, g, 1, 0)
        gk = dot(ds, q, 1, 0)
        acc_v[:plen, :] += gv[:plen]
        acc_v[plen + lo:plen + hi, :] += gv[plen:]
        acc_k[:plen, :] += gk[:plen]
        acc_k[plen + lo:plen + hi, :] += gk[plen:]
        gq = dot(k, ds, 0, 0) * SCALE
        for j in range(GROUP):
            gq_ref[q0:hi, j * D_HEAD:(j + 1) * D_HEAD] = (
                gq[:, j * QB:(j + 1) * QB].T.astype(BF16)
            )


QUARTERS = 4
MESH = pl.DeviceIdType.MESH


def kernel(which_ref, lens_ref, q_ref, g_ref, pk_ref, pv_ref, rk_ref, rv_ref,
           gq_ref, grk_ref, grv_ref, gpk_ref, gpv_ref,
           bias_ref, acc_k, acc_v, buf, cbuf, dbuf, ebuf, fbuf, ids,
           a_send, a_recv, b_send, b_recv, c_send, c_recv, d_send, d_recv,
           e_send, e_recv, i_send, i_recv):
    t = pl.program_id(0)
    planes = buf.shape[3]
    own_rows = pk_ref.shape[0]
    plen = QUARTERS * own_rows
    me = lax.axis_index("dp")
    lo, hi = me % QUARTERS, me // QUARTERS
    core, row = lo % 2, lo // 2
    other_core = me + 1 - 2 * core
    other_row = me + 2 - 4 * row

    def to(src, dst, send, recv, dev):
        return pltpu.make_async_remote_copy(
            src_ref=src, dst_ref=dst, send_sem=send, recv_sem=recv,
            device_id={"dp": dev}, device_id_type=MESH,
        )

    def planes_of(h, j):
        mine = buf.at[h, row, core, hi]
        return to(mine, mine, a_send.at[h, j - 1], a_recv.at[h, j - 1],
                  (hi + j) % planes * QUARTERS + lo)

    def rows_of(h):
        part = buf.at[h, row, core]
        return to(part, part, b_send.at[h], b_recv.at[h], other_row)

    def cores_of(h, r):
        part = buf.at[h, r, core]
        return to(part, part, c_send.at[h, r], c_recv.at[h, r], other_core)

    def quarter_to(h, j):
        peer = (lo + j) % QUARTERS
        return to(cbuf.at[h, peer], dbuf.at[h, lo], d_send.at[h, j - 1], d_recv.at[h, j - 1],
                  hi * QUARTERS + peer)

    def id_to(j):
        return to(ids.at[lo], ids.at[lo], i_send.at[j - 1], i_recv.at[j - 1],
                  hi * QUARTERS + (lo + j) % QUARTERS)

    def term_to(h, j):
        peer = (hi + j) % planes
        return to(ebuf.at[h, peer], fbuf.at[h, hi], e_send.at[h, j - 1], e_recv.at[h, j - 1],
                  peer * QUARTERS + lo)

    def start_rows(h):
        for j in range(1, planes):
            planes_of(h, j).wait_recv()
        rows_of(h).start()

    def start_cores(h):
        rows_of(h).wait_recv()
        for r in range(2):
            cores_of(h, r).start()

    def reduce_group(h):
        for j in range(1, QUARTERS):
            quarter_to(h, j).wait_recv()
        for p in range(planes):
            total = None
            for i in range(QUARTERS):
                flag = jnp.where(ids[i, 0:1, :] == float(p), 1.0, 0.0)
                flag = jnp.concatenate([flag, flag], 1)
                term = dbuf[h, i].astype(F32) * flag
                total = term if total is None else total + term
            ebuf[h, p] = total.astype(BF16)
        fbuf[h, hi] = ebuf[h, hi]
        for j in range(1, planes):
            term_to(h, j).start()

    def reduce_planes(h):
        for j in range(1, planes):
            term_to(h, j).wait_recv()
        total = fbuf[h, 0].astype(F32)
        for p in range(1, planes):
            total = total + fbuf[h, p].astype(F32)
        cols = pl.ds(pl.multiple_of(h * D_HEAD, D_HEAD), D_HEAD)
        gpk_ref[:, cols] = total[:, :D_HEAD].astype(BF16)
        gpv_ref[:, cols] = total[:, D_HEAD:].astype(BF16)

    @pl.when(t == 0)
    def _():
        barrier = pltpu.get_barrier_semaphore()
        for j in range(1, planes):
            pl.semaphore_signal(barrier, inc=1, device_id_type=MESH,
                                device_id={"dp": (hi + j) % planes * QUARTERS + lo})
        for j in range(1, QUARTERS):
            pl.semaphore_signal(barrier, inc=1, device_id_type=MESH,
                                device_id={"dp": hi * QUARTERS + (lo + j) % QUARTERS})
        for h in range(KV_HEADS):
            cols = slice(h * D_HEAD, (h + 1) * D_HEAD)
            buf[h, row, core, hi] = jnp.concatenate([pk_ref[:, cols], pv_ref[:, cols]], 1)
        ids[lo] = jnp.full(ids.shape[1:], which_ref[0], jnp.int32).astype(F32)
        pl.semaphore_wait(barrier, planes - 1 + QUARTERS - 1)

        @pl.loop(0, KV_HEADS)
        def _(h):
            for j in range(1, planes):
                planes_of(h, j).start()

        for j in range(1, QUARTERS):
            id_to(j).start()
        fill_bias([lens_ref[0, i] for i in range(lens_ref.shape[1])], bias_ref)
        start_rows(0)
        start_rows(1)
        start_cores(0)
        for j in range(1, QUARTERS):
            id_to(j).wait()

    @pl.when(t + 2 < KV_HEADS)
    def _():
        start_rows(t + 2)

    @pl.when(t + 1 < KV_HEADS)
    def _():
        start_cores(t + 1)

    for r in range(2):
        cores_of(t, r).wait_recv()
    parts = []
    for i in range(QUARTERS):
        picked = None
        for p in range(planes):
            flag = jnp.where(ids[lo, 0:1, :] == float(p), 1.0, 0.0)
            flag = jnp.concatenate([flag, flag], 1)
            term = buf[t, i // 2, i % 2, p].astype(F32) * flag
            picked = term if picked is None else picked + term
        parts.append(picked.astype(BF16))
    prompt = jnp.concatenate(parts, 0)

    head_grads(q_ref, g_ref, prompt[:, :D_HEAD], prompt[:, D_HEAD:], rk_ref, rv_ref, bias_ref,
               gq_ref, acc_k, acc_v, 0)
    for i in range(QUARTERS):
        rows = slice(i * own_rows, (i + 1) * own_rows)
        cbuf[t, i] = jnp.concatenate([acc_k[rows, :] * SCALE, acc_v[rows, :]], 1).astype(BF16)
    dbuf[t, lo] = cbuf[t, lo]
    for j in range(1, QUARTERS):
        quarter_to(t, j).start()
    grk_ref[...] = (acc_k[plen:, :] * SCALE).astype(BF16)
    grv_ref[...] = acc_v[plen:, :].astype(BF16)

    @pl.when(t >= 1)
    def _():
        reduce_group(t - 1)

    @pl.when(t >= 2)
    def _():
        reduce_planes(t - 2)

    @pl.when(t == KV_HEADS - 1)
    def _():
        reduce_group(KV_HEADS - 1)
        reduce_planes(KV_HEADS - 2)
        reduce_planes(KV_HEADS - 1)

        @pl.loop(0, KV_HEADS)
        def _(h):
            for j in range(1, planes):
                planes_of(h, j).wait_send()
                term_to(h, j).wait_send()
            rows_of(h).wait_send()
            for r in range(2):
                cores_of(h, r).wait_send()
            for j in range(1, QUARTERS):
                quarter_to(h, j).wait_send()


def shards(
    query, resp_key, resp_value, prompt_key, prompt_value, grad_out, resp_lengths, resp_prompt
):
    rows = query.shape[0]
    own_rows = prompt_key.shape[0]
    plen = QUARTERS * own_rows
    width = KV_HEADS * D_HEAD
    planes = lax.axis_size("dp") // QUARTERS
    wide = pl.BlockSpec((rows, GROUP * D_HEAD), lambda h: (0, h))
    own = pl.BlockSpec((rows, D_HEAD), lambda h: (0, h))
    whole = pl.BlockSpec((own_rows, width), lambda h: (0, 0))
    smem = pl.BlockSpec(memory_space=pltpu.SMEM)
    sds = jax.ShapeDtypeStruct
    pair = (own_rows, 2 * D_HEAD)
    dma = pltpu.SemaphoreType.DMA
    return pl.pallas_call(
        kernel,
        grid=(KV_HEADS,),
        in_specs=[smem, smem, wide, wide, whole, whole, own, own],
        out_specs=[wide, own, own, whole, whole],
        scratch_shapes=[
            pltpu.VMEM((rows, rows), F32),
            pltpu.VMEM((plen + rows, D_HEAD), F32),
            pltpu.VMEM((plen + rows, D_HEAD), F32),
            pltpu.VMEM((KV_HEADS, 2, 2, planes) + pair, BF16),
            pltpu.VMEM((KV_HEADS, QUARTERS) + pair, BF16),
            pltpu.VMEM((KV_HEADS, QUARTERS) + pair, BF16),
            pltpu.VMEM((KV_HEADS, planes) + pair, BF16),
            pltpu.VMEM((KV_HEADS, planes) + pair, BF16),
            pltpu.VMEM((QUARTERS, 8, 128), F32),
            dma((KV_HEADS, planes - 1)),
            dma((KV_HEADS, planes - 1)),
            dma((KV_HEADS,)),
            dma((KV_HEADS,)),
            dma((KV_HEADS, 2)),
            dma((KV_HEADS, 2)),
            dma((KV_HEADS, QUARTERS - 1)),
            dma((KV_HEADS, QUARTERS - 1)),
            dma((KV_HEADS, planes - 1)),
            dma((KV_HEADS, planes - 1)),
            dma((QUARTERS - 1,)),
            dma((QUARTERS - 1,)),
        ],
        out_shape=[
            sds((rows, HEADS * D_HEAD), BF16),
            sds((rows, width), BF16),
            sds((rows, width), BF16),
            sds((own_rows, width), BF16),
            sds((own_rows, width), BF16),
        ],
        compiler_params=pltpu.CompilerParams(
            dimension_semantics=("arbitrary",), vmem_limit_bytes=48 * 1024 * 1024,
            collective_id=0, has_side_effects=True,
        ),
    )(resp_prompt, resp_lengths, query, grad_out, prompt_key, prompt_value, resp_key, resp_value)


def solution(mesh):
    rows = P(("groups", "dp"), None)
    return jax.shard_map(
        shards,
        mesh=mesh,
        in_specs=(rows,) * 7 + (P(("groups", "dp")),),
        out_specs=(rows,) * 5,
        check_vma=False,
    )
```

time: 193 us -> 83.8 us (0.43)
  waiting for transfers between devices: 126 us -> 0 us
  Pallas kernels: 37.5 us -> 69.4 us
  between operations: 14.7 us -> 1.3 us
  other arithmetic: 2.75 us -> 0 us
    reduce_scatter x1 -> x0, waiting for transfers between devices: 71.1 us -> none  [shards(): summed = lax.psum_scatter(terms, 'dp', scatter_dimension=0, tiled=True)]
    all_gather x1 -> x0, waiting for transfers between devices: 54.4 us -> none  [shards(): lax.all_gather(jnp.concatenate([prompt_key, prompt_value], 1), 'dp', axis...]
    pallas_call x1, Pallas kernels: 37.5 us -> 69.4 us  [shards(): pl.pallas_call(kernel, grid=(KV_HEADS,), in_specs=[smem, smem, wide, wide...]
    unnamed x10 -> x15, local copies, waits for them, and re-layouts: 7.48 us -> 12.9 us
    broadcast_in_dim x1 -> x0, local copies, waits for them, and re-layouts: 2.47 us -> none  [shards(): terms = jnp.zeros((own_rows * lax.axis_size('dp'), 2 * width), BF16)]
  transfers between devices with their start and end apart: 2 -> 0, of which waited for: 2 -> 0; matrix products, arithmetic and copies ran while one was open for 0% -> 0% of each run, Pallas kernels for 0% -> 0%
where the time goes in v2:
time: 83.8 us; the launch traced here: 83.5 us
  Pallas kernels  69.4 us (83%)
  local copies, waits for them, and re-layouts  12.9 us (15%)
  between operations  1.3 us (2%)
    pallas_call x1, Pallas kernels, shards(): pl.pallas_call(kernel, grid=(KV_HEADS,), in_specs=[smem, smem, wide, wide...  69.4 us
    unnamed x15, local copies, waits for them, and re-layouts  12.9 us

profile of v2, /device:TPU:0, one launch (start us, length us, event | category | flops | bytes accessed | tf_op | source)
XLA Modules:
  0.0 83.5 jit_solution(8175350693336061390)
XLA Ops:
  1.3 0.0 copy-start
  1.3 1.2 %copy-done = bf16[512,1024]{1,0:T(8,128)(2,1)S(1)} copy-done((bf16[512,1024]{1,0:T(8,128)(2,1)S(1)}, bf16[512,1024]{1,0:T(8,128)(2,1)}, u32[]{:S(2)}) %copy-start) | copy-done | bytes 1048600
  2.5 0.0 copy-start.1
  2.5 1.2 %copy-done.1 = bf16[512,1024]{1,0:T(8,128)(2,1)S(1)} copy-done((bf16[512,1024]{1,0:T(8,128)(2,1)S(1)}, bf16[512,1024]{1,0:T(8,128)(2,1)}, u32[]{:S(2)}) %copy-start.1) | copy-done | bytes 1048600
  3.7 0.0 copy-start.2
  3.7 0.9 %copy-done.2 = bf16[64,1024]{1,0:T(8,128)(2,1)S(1)} copy-done((bf16[64,1024]{1,0:T(8,128)(2,1)S(1)}, bf16[64,1024]{1,0:T(8,128)(2,1)}, u32[]{:S(2)}) %copy-start.2) | copy-done | bytes 131096
  4.6 0.0 copy-start.3
  4.6 0.9 %copy-done.3 = bf16[64,1024]{1,0:T(8,128)(2,1)S(1)} copy-done((bf16[64,1024]{1,0:T(8,128)(2,1)S(1)}, bf16[64,1024]{1,0:T(8,128)(2,1)}, u32[]{:S(2)}) %copy-start.3) | copy-done | bytes 131096
  5.5 0.0 copy-start.4
  5.5 0.7 copy-done.4
  6.2 69.4 %shard_map.119 = (bf16[512,4096]{1,0:T(8,128)(2,1)}, bf16[512,1024]{1,0:T(8,128)(2,1)S(1)}, bf16[512,1024]{1,0:T(8,128)(2,1)S(1)}, bf16[64,1024]{1,0:T(8,128)(2,1)S(1)}, bf16[64,1024]{1,0:T(8,128)(2,1)S(1)}) custom-call(s32[1]{0:T(128)S(6)} %copy.18.which_ref, s32[1,4]{1,0:T(1,128)S(1)} %copy-done.4, bf16[512,4096]{1,0:T(8,128)(2,1)} %q_ref.1, ...), custom_call_target="tpu_custom_call" | custom-call | tf_op jit(solution)/shard_map/pallas_call | solution.py:271
  75.6 4.7 %copy.19 = bf16[512,4096]{1,0:T(8,128)(2,1)} copy(bf16[512,4096]{1,0:T(8,128)(2,1)} %get-tuple-element.10) | data formatting | bytes 8388608
  80.3 1.0 %copy.20 = bf16[512,1024]{1,0:T(8,128)(2,1)} copy(bf16[512,1024]{1,0:T(8,128)(2,1)S(1)} %get-tuple-element.11) | data formatting | bytes 2097152
  81.2 1.0 %copy.21 = bf16[512,1024]{1,0:T(8,128)(2,1)} copy(bf16[512,1024]{1,0:T(8,128)(2,1)S(1)} %get-tuple-element.12) | data formatting | bytes 2097152
  82.2 0.7 copy.22
  82.9 0.7 copy.23
Async XLA Ops:
  1.3 1.2 %copy-start = (bf16[512,1024]{1,0:T(8,128)(2,1)S(1)}, bf16[512,1024]{1,0:T(8,128)(2,1)}, u32[]{:S(2)}) copy-start(bf16[512,1024]{1,0:T(8,128)(2,1)} %rk_ref.1) | copy-start | bytes 3145732
  2.5 1.2 %copy-start.1 = (bf16[512,1024]{1,0:T(8,128)(2,1)S(1)}, bf16[512,1024]{1,0:T(8,128)(2,1)}, u32[]{:S(2)}) copy-start(bf16[512,1024]{1,0:T(8,128)(2,1)} %rv_ref.1) | copy-start | bytes 3145732
  3.7 0.9 %copy-start.2 = (bf16[64,1024]{1,0:T(8,128)(2,1)S(1)}, bf16[64,1024]{1,0:T(8,128)(2,1)}, u32[]{:S(2)}) copy-start(bf16[64,1024]{1,0:T(8,128)(2,1)} %pk_ref.1) | copy-start | bytes 393220
  4.6 0.9 %copy-start.3 = (bf16[64,1024]{1,0:T(8,128)(2,1)S(1)}, bf16[64,1024]{1,0:T(8,128)(2,1)}, u32[]{:S(2)}) copy-start(bf16[64,1024]{1,0:T(8,128)(2,1)} %pv_ref.1) | copy-start | bytes 393220
  5.5 0.7 copy-start.4

commit v3 on v2

--- a/solution.py
+++ b/solution.py
@@ -304,7 +304,7 @@
             sds((own_rows, width), BF16),
         ],
         compiler_params=pltpu.CompilerParams(
-            dimension_semantics=("arbitrary",), vmem_limit_bytes=48 * 1024 * 1024,
+            dimension_semantics=("arbitrary",), vmem_limit_bytes=61 * 1024 * 1024,
             collective_id=0, has_side_effects=True,
         ),
     )(resp_prompt, resp_lengths, query, grad_out, prompt_key, prompt_value, resp_key, resp_value)

time: 83.8 us -> 79.1 us (0.944)
  local copies, waits for them, and re-layouts: 12.9 us -> 8.11 us
    unnamed x15 -> x13, local copies, waits for them, and re-layouts: 12.9 us -> 8.11 us
where the time goes in v3:
time: 79.1 us; the launch traced here: 78.9 us
  Pallas kernels  69.5 us (88%)
  local copies, waits for them, and re-layouts  8.11 us (10%)
  between operations  1.31 us (2%)
    pallas_call x1, Pallas kernels, shards(): pl.pallas_call(kernel, grid=(KV_HEADS,), in_specs=[smem, smem, wide, wide...  69.5 us
    unnamed x13, local copies, waits for them, and re-layouts  8.11 us

profile of v3, /device:TPU:0, one launch (start us, length us, event | category | flops | bytes accessed | tf_op | source)
XLA Modules:
  0.0 78.9 jit_solution(11958759713898181897)
XLA Ops:
  1.3 69.5 %shard_map.119 = (bf16[512,4096]{1,0:T(8,128)(2,1)}, bf16[512,1024]{1,0:T(8,128)(2,1)}, bf16[512,1024]{1,0:T(8,128)(2,1)}, bf16[64,1024]{1,0:T(8,128)(2,1)}, bf16[64,1024]{1,0:T(8,128)(2,1)}) custom-call(s32[1]{0:T(128)S(6)} %copy.18.which_ref, s32[1,4]{1,0:T(1,128)} %lens_ref.1, bf16[512,4096]{1,0:T(8,128)(2,1)} %q_ref.1, bf16[512,4096]{1,0:T(8,128)(2,1)} %g_ref.1, ...), custom_call_target="tpu_custom_call" | custom-call | tf_op jit(solution)/shard_map/pallas_call | solution.py:271
  70.8 0.0 copy-start.1
  70.8 0.0 copy-start
  70.8 4.8 %copy.19 = bf16[512,4096]{1,0:T(8,128)(2,1)} copy(bf16[512,4096]{1,0:T(8,128)(2,1)} %get-tuple-element.10) | data formatting | bytes 8388608
  75.7 0.0 copy-done.1
  75.7 0.0 copy-start.3
  75.7 0.0 copy-start.2
  75.7 1.0 %copy.20 = bf16[512,1024]{1,0:T(8,128)(2,1)} copy(bf16[512,1024]{1,0:T(8,128)(2,1)S(1)} %copy-done.1) | data formatting | bytes 2097152
  76.7 0.0 copy-done
  76.7 1.0 %copy.21 = bf16[512,1024]{1,0:T(8,128)(2,1)} copy(bf16[512,1024]{1,0:T(8,128)(2,1)S(1)} %copy-done) | data formatting | bytes 2097152
  77.6 0.0 copy-done.3
  77.6 0.7 copy.22
  78.3 0.0 copy-done.2
  78.3 0.7 copy.23
Async XLA Ops:
  70.8 4.9 %copy-start.1 = (bf16[512,1024]{1,0:T(8,128)(2,1)S(1)}, bf16[512,1024]{1,0:T(8,128)(2,1)}, u32[]{:S(2)}) copy-start(bf16[512,1024]{1,0:T(8,128)(2,1)} %get-tuple-element.11) | copy-start | bytes 3145732
  70.8 5.8 %copy-start = (bf16[512,1024]{1,0:T(8,128)(2,1)S(1)}, bf16[512,1024]{1,0:T(8,128)(2,1)}, u32[]{:S(2)}) copy-start(bf16[512,1024]{1,0:T(8,128)(2,1)} %get-tuple-element.12) | copy-start | bytes 3145732
  75.7 1.9 %copy-start.3 = (bf16[64,1024]{1,0:T(8,128)(2,1)S(1)}, bf16[64,1024]{1,0:T(8,128)(2,1)}, u32[]{:S(2)}) copy-start(bf16[64,1024]{1,0:T(8,128)(2,1)} %get-tuple-element.13) | copy-start | bytes 393220
  75.7 2.6 %copy-start.2 = (bf16[64,1024]{1,0:T(8,128)(2,1)S(1)}, bf16[64,1024]{1,0:T(8,128)(2,1)}, u32[]{:S(2)}) copy-start(bf16[64,1024]{1,0:T(8,128)(2,1)} %get-tuple-element.14) | copy-start | bytes 393220
